TPU v7x, 32 devices: a whole 2x2x4 slice. The times are simulated.
32 devices in a mesh: ctx: 4 (over z), head: 8 (over y, x, core).
Axes of the slice: x: 2, y: 2, z: 4, core: 2. Of those that a mesh axis runs over, the one named last changes fastest.
Arguments:
- out_grad: bfloat16 [1536, 8192], P('ctx', 'head'), may hold values from -0.1796875 to 0.1796875
- conv_input: bfloat16 [1536, 8192], P('ctx', 'head'), may hold values from -0.119628906 to 0.119628906
- residues: float32 [16, 8192], P(None, 'head'), may hold values from -1.5 to 1.5
- decay_rate: float32 [16, 8192], P(None, 'head'), may hold values from 1e-05 to 0.033
- segments: int32 [1536], replicated, may hold values from 0 to 3, never falling along the last dimension, each value on 1 to 768 neighbouring positions
- w_in: bfloat16 [8192, 8192], P('head'), may hold values from -0.0625 to 0.0625
Outputs:
- d_input: bfloat16 [1536, 8192], P('ctx', 'head')
- filter_grad: float32 [16, 8192], P(None, 'head')
Inputs may be any that keep to these rules, and one draw needn't show every extreme that they name: `segments`: document numbers never fall along the tokens; every document has 1 to 768 tokens and one has exactly 768.
All inputs are finite; a program needn't handle non-finite values.
Results may differ from a plain program's by a relative error of at most 0.0049.
Values may be sent and summed in bfloat16 or wider, within the bound.
A program may use at most 128 MiB of HBM per device.

v0:
```python
import math

import jax
import jax.numpy as jnp
from jax import lax
from jax.sharding import PartitionSpec as P


def carried_in(part, axis, combine, identity):
    count = lax.axis_size(axis)
    place = lax.axis_index(axis)
    ahead = count - 1 - place
    gathered = jax.tree.map(lambda a: lax.all_gather(a, axis), part)
    state = jax.tree.map(lambda a, e: jnp.zeros_like(a) + jnp.asarray(e, a.dtype), part, identity)

    def one(hop, state):
        source = count - 1 - hop
        return combine(
            state, jax.tree.map(lambda a: lax.dynamic_index_in_dim(a, source, 0, False), gathered)
        )

    return lax.fori_loop(0, ahead, one, state)


def local(out_grad, conv_input, residues, decay_rate, segments, w_in):
    tok_rows = out_grad.shape[0]
    chan_width = out_grad.shape[1]
    mode_count = residues.shape[0]
    seq_total = segments.shape[0]
    ctx_index = lax.axis_index("ctx")
    row_start = ctx_index * tok_rows
    seg_own = lax.dynamic_slice_in_dim(segments, row_start, tok_rows)
    next_start = jnp.minimum(row_start + tok_rows, seq_total - 1)
    seg_next = lax.dynamic_slice_in_dim(segments, next_start, 1)[0]
    block_len = math.gcd(tok_rows, 32)
    block_count = tok_rows // block_len
    offsets = jnp.arange(block_len, dtype=jnp.float32)
    rising = jnp.exp(-offsets[:, None, None] * decay_rate[None])
    falling = jnp.exp(offsets[:, None, None] * decay_rate[None])
    grad_rows = out_grad.astype(jnp.float32).reshape(block_count, block_len, chan_width)
    weighted = (grad_rows[:, :, None, :] * rising[None]).reshape(
        block_count, block_len, mode_count * chan_width
    )
    seg_blocks = seg_own.reshape(block_count, block_len)
    ahead_mask = jnp.arange(block_len)[None, :] >= jnp.arange(block_len)[:, None]
    upper_mask = (ahead_mask[None] & (seg_blocks[:, :, None] == seg_blocks[:, None, :])).astype(
        jnp.float32
    )
    summed = jnp.einsum("bst,btk->bsk", upper_mask, weighted, precision=lax.Precision.HIGHEST)
    within = summed.reshape(block_count, block_len, mode_count, chan_width) * falling[None]
    next_first = jnp.concatenate([seg_blocks[1:, 0], seg_next[None]])
    linked = (seg_blocks == next_first[:, None]).astype(jnp.float32)
    tail_gain = jnp.exp(-(block_len - offsets)[:, None, None] * decay_rate[None])
    step_decay = jnp.exp(-block_len * decay_rate)

    def chain_step(state, scan_items):
        start_value, start_link = scan_items
        return (start_value + start_link * step_decay * state, state)

    zero_state = jnp.zeros((mode_count, chan_width), jnp.float32)
    head_value, following = lax.scan(
        chain_step, zero_state, (within[:, 0], linked[:, 0]), reverse=True
    )
    local_part = within + linked[:, :, None, None] * tail_gain[None] * following[:, None]
    local_part = local_part.reshape(tok_rows, mode_count, chan_width)
    position = jnp.arange(tok_rows, dtype=jnp.float32)
    reach_mask = (seg_own == seg_next).astype(jnp.float32)
    carry_gain = reach_mask[:, None, None] * jnp.exp(
        -(tok_rows - position)[:, None, None] * decay_rate[None]
    )
    through = jnp.exp(-tok_rows * decay_rate) * (seg_own[0] == seg_next).astype(jnp.float32)
    inputs = conv_input.astype(jnp.float32)
    base_filter = jnp.einsum("sc,smc->mc", inputs, local_part)
    carry_filter = jnp.einsum("sc,smc->mc", inputs, carry_gain)

    def compose(first_part, second_part):
        return (second_part[0] * first_part[0], second_part[1] + second_part[0] * first_part[1])

    unit_state = jnp.ones((mode_count, chan_width), jnp.float32)
    incoming = carried_in((through, head_value), "ctx", compose, (unit_state, zero_state))[1]
    filter_grad = lax.psum(base_filter + carry_filter * incoming, "ctx")
    adjoint = local_part + carry_gain * incoming[None]
    conv_grad = jnp.sum(residues[None] * adjoint, axis=1).astype(jnp.bfloat16)
    d_input = lax.dot_general(
        lax.all_gather(conv_grad, "head", axis=1, tiled=True),
        w_in,
        (((1,), (1,)), ((), ())),
        preferred_element_type=jnp.float32,
    )
    return (d_input.astype(jnp.bfloat16), filter_grad)


def solution(mesh):
    placed = (
        P("ctx", "head"),
        P("ctx", "head"),
        P(None, "head"),
        P(None, "head"),
        P(),
        P("head", None),
    )
    return jax.shard_map(
        local,
        mesh=mesh,
        in_specs=placed,
        out_specs=(P("ctx", "head"), P(None, "head")),
        check_vma=False,
    )
```

profile of v0, /device:TPU:0, one launch (start us, length us, event | category | flops | bytes accessed | tf_op | source)
XLA Modules:
  0.0 256.8 jit_solution(12882592500635488738)
XLA Ops:
  8.0 1.3 dynamic_slice.42
  9.3 1.4 compare_convert_fusion
  11.6 0.7 pad_add_fusion
  13.8 9.7 %mul.212 = f32[12,32,16,1024]{3,2,1,0:T(8,128)} broadcast(bf16[12,32,1024]{2,1,0:T(8,128)(2,1)} %bitcast.89), dimensions={0,1,3} | broadcast | bytes 25952256 | tf_op jit(solution)/shard_map/mul | solution.py:41
  23.6 27.1 %mul.213 = f32[12,32,16384]{2,1,0:T(8,128)} reshape(f32[12,32,16,1024]{3,2,1,0:T(8,128)} %mul.212) | data formatting | bytes 50331648 | tf_op jit(solution)/shard_map/mul | solution.py:41
  51.1 24.2 %fusion.2 = f32[12,32,16384]{2,1,0:T(8,128)} fusion(f32[12,32,16384]{2,1,0:T(8,128)} %mul.213, f32[32,16384]{1,0:T(8,128)S(1)} %multiply_exponential_fusion.2, s32[12,32]{1,0:T(8,128)S(1)} %eq.40, pred[32,32]{1,0:T(8,128)(4,1)S(1)} %iota_compare_fusion), kind=kOutput, calls=%fused_computation.12 | convolution fusion | flops 2422235136 | bytes 52431360 | tf_op jit(solution)/shard_map/bst,btk->bsk/dot_general | solution.py:49
  75.3 25.0 %copy.26 = f32[48,8,16,1024]{3,2,1,0:T(8,128)S(1)} copy(f32[48,8,16,1024]{3,1,2,0:T(8,128)} %bitcast.85) | data formatting | bytes 50331648
  100.3 2.2 multiply_exponential_fusion
  102.6 6.7 %copy-done = f32[48,8,16,1024]{3,2,1,0:T(8,128)} copy-done((f32[48,8,16,1024]{3,2,1,0:T(8,128)}, f32[48,8,16,1024]{3,2,1,0:T(8,128)S(1)}, u32[]{:S(2)}) %copy-start) | copy-done | bytes 25165848
  109.2 0.9 fusion.5
  110.3 25.6 %while.32 = (s32[]{:T(128)}, f32[16,1024]{1,0:T(8,128)S(1)}, f32[12,16,1024]{2,1,0:T(8,128)S(1)}, f32[12,16,1024]{2,1,0:T(8,128)}, f32[12]{0:T(128)S(1)}, /*inde...) while((s32[]{:T(128)}, f32[16,1024]{1,0:T(8,128)S(1)}, f32[12,16,1024]{2,1,0:T(8,128)S(1)}, ...), condition=%wide.region_1.2_spmd.clone, body=%wide.region_0.1_spmd.clone.sunk | while | flops 81924 | bytes 393356 | solution.py:61
  110.3 0.6 dynamic_slice.56
  110.9 1.5 bitcast_add_fusion.2
  112.4 0.6 dynamic_slice.56
  113.0 1.5 bitcast_add_fusion.2
  114.6 0.6 dynamic_slice.56
  115.2 1.5 bitcast_add_fusion.2
  116.7 0.6 dynamic_slice.56
  117.3 1.5 bitcast_add_fusion.2
  118.8 0.6 dynamic_slice.56
  119.4 1.5 bitcast_add_fusion.2
  121.0 0.6 dynamic_slice.56
  121.6 1.5 bitcast_add_fusion.2
  123.1 0.6 dynamic_slice.56
  123.7 1.5 bitcast_add_fusion.2
  125.2 0.6 dynamic_slice.56
  125.8 1.5 bitcast_add_fusion.2
  127.3 0.6 dynamic_slice.56
  127.9 1.5 bitcast_add_fusion.2
  129.5 0.6 dynamic_slice.56
  130.1 1.5 bitcast_add_fusion.2
  131.6 0.6 dynamic_slice.56
  132.2 1.5 bitcast_add_fusion.2
  133.7 0.6 dynamic_slice.56
  134.3 1.5 bitcast_add_fusion.2
  136.0 15.6 %all-gather = f32[64,1024]{1,0:T(8,128)S(1)} all-gather(f32[16,1024]{1,0:T(8,128)S(1)} %get-tuple-element.210), channel_id=2, replica_groups=mesh['ctx'=4,'head'=8] {'ctx'}, dimensions={0}, use_global_device_ids=true | all-gather | bytes 327680 | tf_op jit(solution)/shard_map/all_gather | solution.py:13
  151.6 15.2 %all-gather.1 = f32[64,1024]{1,0:T(8,128)} all-gather(f32[16,1024]{1,0:T(8,128)S(1)} %get-tuple-element.261), channel_id=3, replica_groups=mesh['ctx'=4,'head'=8] {'ctx'}, dimensions={0}, use_global_device_ids=true | all-gather | bytes 327680 | tf_op jit(solution)/shard_map/all_gather | solution.py:13
  166.9 2.9 %while.31 = (s32[]{:T(128)}, f32[16,1024]{1,0:T(8,128)S(1)}, s32[]{:T(128)}, f32[4,16,1024]{2,1,0:T(8,128)S(1)}, f32[4,16,1024]{2,1,0:T(8,128)}, /*index=5*/s32[]{:T(128)}, s32[]{:T(128)}, s32[]{:T(128)}, s32[]{:T(128)}) while((s32[]{:T(128)}, f32[16,1024]{1,0:T(8,128)S(1)}, s32[]{:T(128)}, f32[4,16,1024]{2,1,0:T(8,128)S(1)}, ...), condition=%wide.region_3.4_spmd, body=%wide.region_2.3_spmd.sunk | while | flops 32774 | bytes 262287 | solution.py:22
  166.9 0.9 fusion.15
  167.8 0.9 fusion.15
  168.7 0.9 fusion.15
  169.8 21.3 %multiply_reduce_fusion.2 = bf16[384,1024]{1,0:T(8,128)(2,1)} fusion(f32[16,1024]{1,0:T(8,128)S(1)} %get-tuple-element.211, f32[16,1024]{1,0:T(8,128)S(1)} %copy-done.1, f32[384]{0:T(512)S(1)} %subtract_negate_fusion, f32[384]{0:T(512)S(1)} %get-tuple-element.257, f32[12,16,1024]{2,1,0:T(8,128)S(1)} %get-tuple-element.209, f32[48,8,16,1024]{3,2,1,0:T(8,128)} %copy-done, ...), kind=kLoop, calls=%fused_computation.10 | loop fusion | flops 62521344 | bytes 31134208 | tf_op jit(solution)/shard_map/reduce_sum | solution.py:83
  191.1 1.3 bitcast_convert_fusion
  192.4 17.0 %multiply_reduce_fusion.1 = (f32[1024,16]{0,1:T(8,128)S(1)}, f32[1024,16]{0,1:T(8,128)S(1)}) fusion(f32[1024,384]{0,1:T(8,128)S(1)} %bitcast_convert_fusion, f32[12,16,1024]{2,1,0:T(8,128)S(1)} %get-tuple-element.209, f32[48,8,16,1024]{3,2,1,0:T(8,128)} %copy-done, f32[32,16,1024]{2,1,0:T(8,128)} %get-tuple-element.259, f32[384]{0:T(512)S(1)} %compare_convert_fusion.1, ...), kind=kLoop, calls=%fused_computation.9 | loop fusion | flops 62881792 | bytes 31920640 | tf_op jit(solution)/shard_map/sc,smc->mc/dot_general | solution.py:73
  209.5 0.6 fusion.11
  210.1 24.9 %all-gather.4.cloned.1.call-done = bf16[384,8192]{1,0:T(8,128)(2,1)} async-done(((bf16[384,1024]{1,0:T(8,128)(2,1)}), bf16[384,8192]{1,0:T(8,128)(2,1)}) %all-gather.4.cloned.1.call-update) | async-done | bytes 6291472 | tf_op jit(solution)/shard_map/all_gather | solution.py:85
  235.0 12.8 %convolution_convert_fusion = bf16[384,1024]{1,0:T(8,128)(2,1)} fusion(bf16[384,8192]{1,0:T(8,128)(2,1)} %all-gather.4.cloned.1.call-done, bf16[1024,8192]{1,0:T(8,128)(2,1)} %param.15), kind=kOutput, calls=%fused_computation.18 | convolution fusion | flops 6442844160 | bytes 23855104 | tf_op jit(solution)/shard_map/dot_general | solution.py:84
  247.9 1.5 copy.45
  (40 shorter events, 1.9 us)
Async XLA Ops:
  8.0 227.0 %all-gather.4.cloned.1.call-start = ((), (), s32[]{:S(2)}) async-start(), calls=%async_computation | async-start | bytes 7077888 | tf_op jit(solution)/shard_map/all_gather | solution.py:85
  23.6 27.1 %copy-start.1 = (f32[16,1024]{1,0:T(8,128)S(1)}, f32[16,1024]{1,0:T(8,128)}, u32[]{:S(2)}) copy-start(f32[16,1024]{1,0:T(8,128)} %param.13) | copy-start | bytes 196612
  75.3 94.4 %copy-start.2 = (f32[16,1024]{1,0:T(8,128)S(1)}, f32[16,1024]{1,0:T(8,128)}, u32[]{:S(2)}) copy-start(f32[16,1024]{1,0:T(8,128)} %param.12) | copy-start | bytes 196612
  100.3 8.9 %copy-start = (f32[48,8,16,1024]{3,2,1,0:T(8,128)}, f32[48,8,16,1024]{3,2,1,0:T(8,128)S(1)}, u32[]{:S(2)}) copy-start(f32[48,8,16,1024]{3,2,1,0:T(8,128)S(1)} %copy.26) | copy-start | bytes 75497472
  191.1 56.8 %all-reduce.2.cloned.1.call-start = ((), (), s32[]{:S(2)}) async-start(), calls=%async_computation.1 | async-start | bytes 131072 | tf_op jit(solution)/shard_map/psum | solution.py:81
Sparse Core Ops, SparseCore 0:
  191.2 43.7 all-gather.3
Sparse Core Ops, SparseCore 1:
  210.2 32.2 all-reduce.1
where the time goes:
time: 259 us; the launch traced here: 257 us
  local copies, waits for them, and re-layouts  79.5 us (31%)
  other arithmetic  66.9 us (26%)
  matrix products  37 us (14%)
  blocking collectives  30.8 us (12%)
  waiting for transfers between devices  24.9 us (10%)
  between operations  16.9 us (7%)
    mul x2, local copies, waits for them, and re-layouts, local(): grad_rows[:, :, None, :] * rising[None]  36.8 us
    unnamed x9, local copies, waits for them, and re-layouts  33.1 us
    all_gather x2, blocking collectives, carried_in(): gathered = jax.tree.map(lambda a: lax.all_gather(a, axis), part)  30.8 us
    all_gather x1, waiting for transfers between devices, local(): lax.all_gather(conv_grad, 'head', axis=1, tiled=True)  24.9 us
    dot_general x1, matrix products, local(): jnp.einsum('bst,btk->bsk', upper_mask, weighted, precision=lax.Precision....  24.2 us
    reduce_sum x1, other arithmetic, local(): conv_grad = jnp.sum(residues[None] * adjoint, axis=1).astype(jnp.bfloat16)  21.3 us
    add x12, other arithmetic, chain_step(): return (start_value + start_link * step_decay * state, state)  17.9 us
    dot_general x1, other arithmetic, local(): base_filter = jnp.einsum('sc,smc->mc', inputs, local_part)  17 us
  transfers between devices with their start and end apart: 2, of which 1 were waited for; matrix products, arithmetic and copies ran while one was open for 12% of the time, Pallas kernels for 0%

commit v1 on v0

v1 whole, which is shorter than its diff:
```python
import functools

import jax
import jax.numpy as jnp
from jax import lax
from jax.experimental import pallas as pl
from jax.experimental.pallas import tpu as pltpu
from jax.sharding import PartitionSpec as P

LANES = 128
VMEM = pl.BlockSpec(memory_space=pltpu.VMEM)
SMEM = pl.BlockSpec(memory_space=pltpu.SMEM)


def spread(src, dst, convert):
    rows, width = src.shape
    for tile in range(width // LANES):
        dst[pl.ds(tile * rows, rows), :] = convert(src[:, pl.ds(tile * LANES, LANES)])


def fold(src, dst, convert):
    rows, width = dst.shape
    for tile in range(width // LANES):
        dst[:, pl.ds(tile * LANES, LANES)] = convert(src[pl.ds(tile * rows, rows), :])


def wide(value):
    return value.astype(jnp.float32)


def fill_decay(rate_ref, mode_scr, decay_scr):
    modes = rate_ref.shape[0]
    subs = rate_ref.shape[1] // LANES
    spread(rate_ref, mode_scr, lambda v: jnp.exp(-v))
    for m in range(modes):
        decay_scr[0, m] = jnp.zeros((subs, LANES), jnp.float32)
        decay_scr[1, m] = mode_scr[pl.ds(m, subs, stride=modes), :]


def link_at(seg_ref, token):
    last = seg_ref.shape[0] - 1
    same = seg_ref[token] == seg_ref[jnp.minimum(token + 1, last)]
    return jnp.where(same, 1, 0)


def head_kernel(seg_ref, grad_ref, rate_ref, out_ref, grad_scr, mode_scr, decay_scr):
    rows, width = grad_ref.shape
    modes = rate_ref.shape[0]
    subs = width // LANES
    start = lax.axis_index("ctx") * rows
    spread(grad_ref, grad_scr, wide)
    fill_decay(rate_ref, mode_scr, decay_scr)

    def step(i, state):
        t = rows - 1 - i
        link = link_at(seg_ref, start + t)
        grad = grad_scr[pl.ds(t, subs, stride=rows), :]
        return tuple(grad + decay_scr[link, m] * state[m] for m in range(modes))

    zero = jnp.zeros((subs, LANES), jnp.float32)
    state = lax.fori_loop(0, rows, step, (zero,) * modes, unroll=8)
    for m in range(modes):
        out_ref[m] = state[m]


def main_kernel(
    seg_ref, grad_ref, input_ref, residue_ref, rate_ref, heads_ref,
    conv_ref, filter_ref,
    grad_scr, input_scr, conv_scr, mode_scr, through_scr, decay_scr, residue_scr, carry_scr,
):
    rows, width = grad_ref.shape
    modes = rate_ref.shape[0]
    subs = width // LANES
    place = lax.axis_index("ctx")
    count = heads_ref.shape[0]
    start = place * rows
    spread(grad_ref, grad_scr, wide)
    spread(input_ref, input_scr, wide)
    spread(residue_ref, mode_scr, lambda v: v)
    for m in range(modes):
        residue_scr[m] = mode_scr[pl.ds(m, subs, stride=modes), :]
    spread(rate_ref, mode_scr, lambda v: jnp.exp(-rows * v))
    for m in range(modes):
        through_scr[m] = mode_scr[pl.ds(m, subs, stride=modes), :]
    fill_decay(rate_ref, mode_scr, decay_scr)
    carry_scr[...] = jnp.zeros_like(carry_scr)
    last = seg_ref.shape[0] - 1

    def hop(i, carry):
        source = count - 1 - i
        same = seg_ref[source * rows] == seg_ref[jnp.minimum((source + 1) * rows, last)]
        linked = jnp.where(same, 1.0, 0.0)
        carry_scr[...] = heads_ref[source] + linked * through_scr[...] * carry_scr[...]
        return carry

    lax.fori_loop(0, count - 1 - place, hop, 0)

    def step(i, state):
        values, sums = state
        t = rows - 1 - i
        link = link_at(seg_ref, start + t)
        grad = grad_scr[pl.ds(t, subs, stride=rows), :]
        inputs = input_scr[pl.ds(t, subs, stride=rows), :]
        values = tuple(grad + decay_scr[link, m] * values[m] for m in range(modes))
        sums = tuple(sums[m] + inputs * values[m] for m in range(modes))
        parts = [residue_scr[m] * values[m] for m in range(modes)]
        while len(parts) > 1:
            parts = [a + b for a, b in zip(parts[::2], parts[1::2])]
        conv_scr[pl.ds(t, subs, stride=rows), :] = parts[0]
        return values, sums

    zero = jnp.zeros((subs, LANES), jnp.float32)
    values = tuple(carry_scr[m] for m in range(modes))
    _, sums = lax.fori_loop(0, rows, step, (values, (zero,) * modes), unroll=4)
    for m in range(modes):
        mode_scr[pl.ds(m, subs, stride=modes), :] = sums[m]
    fold(mode_scr, filter_ref, lambda v: v)
    fold(conv_scr, conv_ref, lambda v: v.astype(conv_ref.dtype))


def local(out_grad, conv_input, residues, decay_rate, segments, w_in):
    rows, width = out_grad.shape
    modes = residues.shape[0]
    subs = width // LANES
    f32 = jnp.float32
    tall = pltpu.VMEM((rows * subs, LANES), f32)
    flat = pltpu.VMEM((modes * subs, LANES), f32)
    packed = pltpu.VMEM((modes, subs, LANES), f32)
    decays = pltpu.VMEM((2, modes, subs, LANES), f32)
    params = pltpu.CompilerParams(vmem_limit_bytes=32 << 20)
    head = pl.pallas_call(
        head_kernel,
        out_shape=jax.ShapeDtypeStruct((modes, subs, LANES), f32),
        in_specs=[SMEM, VMEM, VMEM],
        out_specs=VMEM,
        scratch_shapes=[tall, flat, decays],
        compiler_params=params,
        name="head_state",
    )(segments, out_grad, decay_rate)
    heads = lax.all_gather(head, "ctx")
    conv_grad, partial = pl.pallas_call(
        main_kernel,
        out_shape=(
            jax.ShapeDtypeStruct((rows, width), jnp.bfloat16),
            jax.ShapeDtypeStruct((modes, width), f32),
        ),
        in_specs=[SMEM] + [VMEM] * 5,
        out_specs=(VMEM, VMEM),
        scratch_shapes=[tall, tall, tall, flat, packed, decays, packed, packed],
        compiler_params=params,
        name="adjoint_scan",
    )(segments, out_grad, conv_input, residues, decay_rate, heads)
    filter_grad = lax.psum(partial, "ctx")
    d_input = lax.dot_general(
        lax.all_gather(conv_grad, "head", axis=1, tiled=True),
        w_in,
        (((1,), (1,)), ((), ())),
        preferred_element_type=f32,
    )
    return (d_input.astype(jnp.bfloat16), filter_grad)


def solution(mesh):
    placed = (
        P("ctx", "head"),
        P("ctx", "head"),
        P(None, "head"),
        P(None, "head"),
        P(),
        P("head", None),
    )
    return jax.shard_map(
        local,
        mesh=mesh,
        in_specs=placed,
        out_specs=(P("ctx", "head"), P(None, "head")),
        check_vma=False,
    )
```

time: 259 us -> 112 us (0.43)
  local copies, waits for them, and re-layouts: 79.5 us -> 6.11 us
  other arithmetic: 66.9 us -> 0 us
  matrix products: 37 us -> 12.8 us
  waiting for transfers between devices: 24.9 us -> 47.1 us
  blocking collectives: 30.8 us -> 15.6 us
  Pallas kernels: 0 us -> 14.1 us
    mul x2 -> x0, local copies, waits for them, and re-layouts: 36.8 us -> none  [local(): grad_rows[:, :, None, :] * rising[None]]
    unnamed x9 -> x11, local copies, waits for them, and re-layouts: 33.1 us -> 6.11 us
    dot_general x1 -> x0, matrix products: 24.2 us -> none  [local(): jnp.einsum('bst,btk->bsk', upper_mask, weighted, precision=lax.Precision....]
    all_gather x1, waiting for transfers between devices: 24.9 us -> 46.6 us  [local(): lax.all_gather(conv_grad, 'head', axis=1, tiled=True)]
    reduce_sum x1 -> x0, other arithmetic: 21.3 us -> none  [local(): conv_grad = jnp.sum(residues[None] * adjoint, axis=1).astype(jnp.bfloat16)]
    add x16 -> x0, other arithmetic: 21.2 us -> none  [the longest x12 17.9 us: chain_step(): return (start_value + start_link * step_decay * state, state)]
    dot_general x1 -> x0, other arithmetic: 17 us -> none  [local(): base_filter = jnp.einsum('sc,smc->mc', inputs, local_part)]
    all_gather x2 -> x1, blocking collectives: 30.8 us -> 15.6 us  [local(): heads = lax.all_gather(head, 'ctx')]
where the time goes in v1:
time: 112 us; the launch traced here: 111 us
  waiting for transfers between devices  47.1 us (42%)
  blocking collectives  15.6 us (14%)
  between operations  15.5 us (14%)
  Pallas kernels  14.1 us (13%)
  matrix products  12.8 us (11%)
  local copies, waits for them, and re-layouts  6.11 us (5%)
    all_gather x1, waiting for transfers between devices, local(): lax.all_gather(conv_grad, 'head', axis=1, tiled=True)  46.6 us
    all_gather x1, blocking collectives, local(): heads = lax.all_gather(head, 'ctx')  15.6 us
    dot_general x1, matrix products, local(): lax.dot_general(lax.all_gather(conv_grad, 'head', axis=1, tiled=True), w_...  12.8 us
    pallas_call x1, Pallas kernels, local(): pl.pallas_call(main_kernel, out_shape=(jax.ShapeDtypeStruct((rows, width)...  10.3 us
    unnamed x11, local copies, waits for them, and re-layouts  6.11 us
    pallas_call x1, Pallas kernels, local(): pl.pallas_call(head_kernel, out_shape=jax.ShapeDtypeStruct((modes, subs,...  3.8 us
  transfers between devices with their start and end apart: 2, of which 1 were waited for; matrix products, arithmetic and copies ran while one was open for 12% of the time, Pallas kernels for 0%

profile of v1, /device:TPU:0, one launch (start us, length us, event | category | flops | bytes accessed | tf_op | source)
XLA Modules:
  0.0 111.4 jit_solution(4781578352616073598)
XLA Ops:
  8.0 0.0 all-gather.3.cloned.1.call-start
  8.0 0.0 copy-start
  8.1 1.1 %copy-done = bf16[384,1024]{1,0:T(8,128)(2,1)S(1)} copy-done((bf16[384,1024]{1,0:T(8,128)(2,1)S(1)}, bf16[384,1024]{1,0:T(8,128)(2,1)}, u32[]{:S(2)}) %copy-start) | copy-done | bytes 786456
  9.2 0.0 copy-start.2
  9.2 0.8 copy-done.2
  10.0 0.0 copy-start.4
  10.0 0.7 copy-done.4
  10.7 3.8 %head_state.1 = f32[16,8,128]{2,1,0:T(8,128)S(1)} custom-call(s32[1536]{0:T(1024)S(1)} %copy-done.4, bf16[384,1024]{1,0:T(8,128)(2,1)S(1)} %copy-done, f32[16,1024]{1,0:T(8,128)S(1)} %copy-done.2), custom_call_target="tpu_custom_call" | custom-call | tf_op jit(solution)/shard_map/head_state/pallas_call | solution.py:131
  14.5 15.6 %all-gather = f32[64,8,128]{2,1,0:T(8,128)S(1)} all-gather(f32[16,8,128]{2,1,0:T(8,128)S(1)} %head_state.1), channel_id=2, replica_groups=mesh['ctx'=4,'head'=8] {'ctx'}, dimensions={0}, use_global_device_ids=true | all-gather | bytes 327680 | tf_op jit(solution)/shard_map/all_gather | solution.py:140
  30.1 0.0 copy-start.1
  30.1 1.1 %copy-done.1 = bf16[384,1024]{1,0:T(8,128)(2,1)S(1)} copy-done((bf16[384,1024]{1,0:T(8,128)(2,1)S(1)}, bf16[384,1024]{1,0:T(8,128)(2,1)}, u32[]{:S(2)}) %copy-start.1) | copy-done | bytes 786456
  31.3 0.0 copy-start.3
  31.3 0.8 copy-done.3
  32.1 10.3 %adjoint_scan.1 = (bf16[384,1024]{1,0:T(8,128)(2,1)}, f32[16,1024]{1,0:T(8,128)}) custom-call(s32[1536]{0:T(1024)S(1)} %copy-done.4, bf16[384,1024]{1,0:T(8,128)(2,1)S(1)} %copy-done, bf16[384,1024]{1,0:T(8,128)(2,1)S(1)} %copy-done.1, f32[16,1024]{1,0:T(8,128)S(1)} %copy-done.3, f32[16,1024]{1,0:T(8,128)S(1)} %copy-done.2, f32[4,16,8,128]{3,2,1,0:T(8,128)S(1)} %bitcast.3), custom_call_target="tpu_custom_call" | custom-call | tf_op jit(solution)/shard_map/adjoint_scan/pallas_call | solution.py:141
  42.4 0.0 all-gather.3.cloned.1.call-update
  42.5 0.0 all-reduce.2.cloned.1.call-start
  42.5 0.5 all-reduce.2.cloned.1.call-update
  43.0 46.6 %all-gather.3.cloned.1.call-done = bf16[384,8192]{1,0:T(8,128)(2,1)} async-done(((bf16[384,1024]{1,0:T(8,128)(2,1)}), bf16[384,8192]{1,0:T(8,128)(2,1)}) %all-gather.3.cloned.1.call-update) | async-done | bytes 6291472 | tf_op jit(solution)/shard_map/all_gather | solution.py:155
  89.6 12.8 %convolution_convert_fusion = bf16[384,1024]{1,0:T(8,128)(2,1)} fusion(bf16[384,8192]{1,0:T(8,128)(2,1)} %all-gather.3.cloned.1.call-done, bf16[1024,8192]{1,0:T(8,128)(2,1)} %param.11), kind=kOutput, calls=%fused_computation | convolution fusion | flops 6442844160 | bytes 23855104 | tf_op jit(solution)/shard_map/dot_general | solution.py:154
  102.4 0.0 all-reduce.2.cloned.1.call-done
  102.5 1.5 %copy.9 = f32[16,1024]{1,0:T(8,128)} copy(f32[16,1024]{1,0:T(8,128)} %all-reduce.2.cloned.1.call-done) | data formatting | bytes 131072
Async XLA Ops:
  8.0 81.6 %all-gather.3.cloned.1.call-start = ((), (), s32[]{:S(2)}) async-start(), calls=%async_computation | async-start | bytes 7077888 | tf_op jit(solution)/shard_map/all_gather | solution.py:155
  8.0 1.1 %copy-start = (bf16[384,1024]{1,0:T(8,128)(2,1)S(1)}, bf16[384,1024]{1,0:T(8,128)(2,1)}, u32[]{:S(2)}) copy-start(bf16[384,1024]{1,0:T(8,128)(2,1)} %grad_ref.3) | copy-start | bytes 2359300
  9.2 0.8 copy-start.2
  10.0 0.7 copy-start.4
  30.1 1.1 %copy-start.1 = (bf16[384,1024]{1,0:T(8,128)(2,1)S(1)}, bf16[384,1024]{1,0:T(8,128)(2,1)}, u32[]{:S(2)}) copy-start(bf16[384,1024]{1,0:T(8,128)(2,1)} %input_ref.1) | copy-start | bytes 2359300
  31.3 0.8 copy-start.3
  42.5 60.0 %all-reduce.2.cloned.1.call-start = ((), (), s32[]{:S(2)}) async-start(), calls=%async_computation.1 | async-start | bytes 131072 | tf_op jit(solution)/shard_map/psum | solution.py:153
Sparse Core Ops, SparseCore 0:
  42.6 47.0 all-gather.2
Sparse Core Ops, SparseCore 1:
  45.8 35.3 all-reduce.1

commit v2 on v1

--- a/solution.py
+++ b/solution.py
@@ -9,6 +9,7 @@
 
 LANES = 128
 VMEM = pl.BlockSpec(memory_space=pltpu.VMEM)
+MESH = pl.DeviceIdType.MESH
 SMEM = pl.BlockSpec(memory_space=pltpu.SMEM)
 
 
@@ -90,7 +91,7 @@
         source = count - 1 - i
         same = seg_ref[source * rows] == seg_ref[jnp.minimum((source + 1) * rows, last)]
         linked = jnp.where(same, 1.0, 0.0)
-        carry_scr[...] = heads_ref[source] + linked * through_scr[...] * carry_scr[...]
+        carry_scr[...] = heads_ref[source - place] + linked * through_scr[...] * carry_scr[...]
         return carry
 
     lax.fori_loop(0, count - 1 - place, hop, 0)
@@ -116,6 +117,220 @@
         mode_scr[pl.ds(m, subs, stride=modes), :] = sums[m]
     fold(mode_scr, filter_ref, lambda v: v)
     fold(conv_scr, conv_ref, lambda v: v.astype(conv_ref.dtype))
+
+
+def exchange_kernel(head_ref, out_ref, send_sem, recv_sem):
+    count = out_ref.shape[0]
+    place = lax.axis_index("ctx")
+    out_ref[...] = jnp.zeros_like(out_ref)
+    barrier = pltpu.get_barrier_semaphore()
+    for d in range(1, count):
+        other = lax.rem(place + d, count)
+        pl.semaphore_signal(barrier, inc=1, device_id={"ctx": other}, device_id_type=MESH)
+    pl.semaphore_wait(barrier, count - 1)
+    copies = []
+    for d in range(1, count):
+        other = jnp.maximum(place - d, 0)
+        copies.append(pltpu.make_async_remote_copy(
+            src_ref=head_ref,
+            dst_ref=out_ref.at[d],
+            send_sem=send_sem.at[d],
+            recv_sem=recv_sem.at[d],
+            device_id={"ctx": other},
+            device_id_type=MESH,
+        ))
+    for d in range(1, count):
+        pl.when(place >= d)(copies[d - 1].start)
+    for d in range(1, count):
+        pl.when(place >= d)(copies[d - 1].wait_send)
+        pl.when(place + d < count)(copies[d - 1].wait_recv)
+
+
+def gather_kernel(
+    conv_ref, w_ref, part_ref, out_ref, filter_ref,
+    blocks, weights, total, parts,
+    send_sem, recv_sem, weight_sem, part_send, part_recv,
+):
+    rows, width = conv_ref.shape
+    half = rows // 2
+    count = parts.shape[0]
+    place = lax.axis_index("ctx")
+    me = lax.axis_index("head")
+    core = lax.rem(me, 2)
+    east = lax.rem(me // 2, 2)
+    north = me // 4
+    steps = {1: 1 - 2 * core, 2: 2 - 4 * east, 4: 4 - 8 * north}
+
+    def apart(k):
+        return me + sum(steps[bit] for bit in steps if k & bit)
+
+    loads = []
+    for k in range(8):
+        loads.append(pltpu.make_async_copy(
+            w_ref.at[:, pl.ds(pl.multiple_of(apart(k) * width, LANES), width)],
+            weights.at[k],
+            weight_sem.at[k],
+        ))
+        loads[k].start()
+
+    barrier = pltpu.get_barrier_semaphore()
+    for bit in steps:
+        pl.semaphore_signal(barrier, inc=1, device_id={"head": apart(bit)}, device_id_type=MESH)
+    for d in range(1, count):
+        other = lax.rem(place + d, count)
+        pl.semaphore_signal(barrier, inc=1, device_id={"ctx": other}, device_id_type=MESH)
+    pl.semaphore_wait(barrier, 3 + count - 1)
+
+    def piece(k, h):
+        if k == 0:
+            return conv_ref.at[pl.ds(h * half, half)]
+        return blocks.at[k - 1, pl.ds(h * half, half)]
+
+    sent = {}
+
+    def send(k, h, bit):
+        copy = pltpu.make_async_remote_copy(
+            src_ref=piece(k, h),
+            dst_ref=piece(k ^ bit, h),
+            send_sem=send_sem.at[(k ^ bit) - 1, h],
+            recv_sem=recv_sem.at[(k ^ bit) - 1, h],
+            device_id={"head": apart(bit)},
+            device_id_type=MESH,
+        )
+        copy.start()
+        sent[k ^ bit, h] = copy
+
+    def multiply(k, first, size):
+        def tile(n, carry):
+            columns = pl.ds(pl.multiple_of(n * 256, 256), 256)
+            source = conv_ref if k == 0 else blocks.at[k - 1]
+            product = lax.dot_general(
+                source[pl.ds(first, size), :],
+                weights[k, columns, :],
+                (((1,), (1,)), ((), ())),
+                preferred_element_type=jnp.float32,
+            )
+            if k == 0:
+                total[pl.ds(first, size), columns] = product
+            else:
+                total[pl.ds(first, size), columns] += product
+            return carry
+
+        lax.fori_loop(0, total.shape[1] // 256, tile, 0)
+
+    send(0, 0, 2)
+    send(0, 1, 4)
+    send(0, 1, 2)
+    send(0, 0, 4)
+    send(0, 0, 1)
+    send(0, 1, 1)
+    sums = []
+    for d in range(1, count):
+        other = lax.rem(place + d, count)
+        sums.append(pltpu.make_async_remote_copy(
+            src_ref=part_ref,
+            dst_ref=parts.at[count - d],
+            send_sem=part_send.at[d],
+            recv_sem=part_recv.at[count - d],
+            device_id={"ctx": other},
+            device_id_type=MESH,
+        ))
+        sums[-1].start()
+    parts[0] = part_ref[...]
+    loads[0].wait()
+    multiply(0, 0, rows)
+    sent[1, 0].wait_recv()
+    sent[1, 1].wait_recv()
+    loads[1].wait()
+    multiply(1, 0, rows)
+    sent[2, 0].wait_recv()
+    send(2, 0, 4)
+    send(2, 0, 1)
+    sent[4, 1].wait_recv()
+    send(4, 1, 2)
+    send(4, 1, 1)
+    for k in (2, 3, 4, 5):
+        loads[k].wait()
+    multiply(2, 0, half)
+    multiply(4, half, half)
+    sent[3, 0].wait_recv()
+    multiply(3, 0, half)
+    sent[5, 1].wait_recv()
+    multiply(5, half, half)
+    for copy in sums:
+        copy.wait()
+    value = parts[lax.rem(count - place, count)]
+    for z in range(1, count):
+        value = value + parts[lax.rem(z + count - place, count)]
+    filter_ref[...] = value
+    sent[2, 1].wait_recv()
+    send(2, 1, 1)
+    sent[4, 0].wait_recv()
+    send(4, 0, 1)
+    multiply(2, half, half)
+    multiply(4, 0, half)
+    sent[3, 1].wait_recv()
+    multiply(3, half, half)
+    sent[5, 0].wait_recv()
+    multiply(5, 0, half)
+    sent[6, 0].wait_recv()
+    send(6, 0, 1)
+    sent[6, 1].wait_recv()
+    send(6, 1, 1)
+    loads[6].wait()
+    multiply(6, 0, rows)
+    sent[7, 0].wait_recv()
+    sent[7, 1].wait_recv()
+    loads[7].wait()
+    multiply(7, 0, rows)
+    for copy in sent.values():
+        copy.wait_send()
+    out_ref[...] = total[...].astype(out_ref.dtype)
+
+
+def exchange(head):
+    count = lax.axis_size("ctx")
+    return pl.pallas_call(
+        exchange_kernel,
+        out_shape=jax.ShapeDtypeStruct((count,) + head.shape, head.dtype),
+        in_specs=[VMEM],
+        out_specs=VMEM,
+        scratch_shapes=[pltpu.SemaphoreType.DMA((count,))] * 2,
+        compiler_params=pltpu.CompilerParams(collective_id=1, has_side_effects=True),
+        name="head_exchange",
+    )(head)
+
+
+def gather_multiply(conv_grad, w_in, partial):
+    rows, width = conv_grad.shape
+    features = w_in.shape[0]
+    count = lax.axis_size("ctx")
+    dma = pltpu.SemaphoreType.DMA
+    return pl.pallas_call(
+        gather_kernel,
+        out_shape=(
+            jax.ShapeDtypeStruct((rows, features), jnp.bfloat16),
+            jax.ShapeDtypeStruct(partial.shape, partial.dtype),
+        ),
+        in_specs=[VMEM, pl.BlockSpec(memory_space=pl.ANY), VMEM],
+        out_specs=(VMEM, VMEM),
+        scratch_shapes=[
+            pltpu.VMEM((7, rows, width), jnp.bfloat16),
+            pltpu.VMEM((8, features, width), jnp.bfloat16),
+            pltpu.VMEM((rows, features), jnp.float32),
+            pltpu.VMEM((count,) + partial.shape, partial.dtype),
+            dma((7, 2)), dma((7, 2)), dma((8,)), dma((count,)), dma((count,)),
+        ],
+        compiler_params=pltpu.CompilerParams(
+            collective_id=2, has_side_effects=True, vmem_limit_bytes=44 << 20
+        ),
+        cost_estimate=pl.CostEstimate(
+            flops=16 * rows * width * features,
+            bytes_accessed=16 * features * width,
+            transcendentals=0,
+        ),
+        name="gather_multiply",
+    )(conv_grad, w_in, partial)
 
 
 def local(out_grad, conv_input, residues, decay_rate, segments, w_in):
@@ -137,7 +352,7 @@
         compiler_params=params,
         name="head_state",
     )(segments, out_grad, decay_rate)
-    heads = lax.all_gather(head, "ctx")
+    heads = exchange(head)
     conv_grad, partial = pl.pallas_call(
         main_kernel,
         out_shape=(
@@ -150,6 +365,8 @@
         compiler_params=params,
         name="adjoint_scan",
     )(segments, out_grad, conv_input, residues, decay_rate, heads)
+    if lax.axis_size("head") == 8:
+        return gather_multiply(conv_grad, w_in, partial)
     filter_grad = lax.psum(partial, "ctx")
     d_input = lax.dot_general(
         lax.all_gather(conv_grad, "head", axis=1, tiled=True),

time: 112 us -> 70.4 us (0.63)
  waiting for transfers between devices: 47.1 us -> 0 us
  Pallas kernels: 14.1 us -> 58.6 us
  blocking collectives: 15.6 us -> 0 us
  between operations: 15.5 us -> 0.69 us
  matrix products: 12.8 us -> 0 us
  local copies, waits for them, and re-layouts: 6.11 us -> 10.4 us
    all_gather x1 -> x0, waiting for transfers between devices: 46.6 us -> none  [local(): lax.all_gather(conv_grad, 'head', axis=1, tiled=True)]
    pallas_call x0 -> x2, Pallas kernels: none -> 45.3 us  [the longest x1 32.1 us: gather_multiply(): pl.pallas_call(gather_kernel, out_shape=(jax.ShapeDtypeStruct((rows, feat...]
    all_gather x1 -> x0, blocking collectives: 15.6 us -> none  [local(): heads = lax.all_gather(head, 'ctx')]
    dot_general x1 -> x0, matrix products: 12.8 us -> none  [local(): lax.dot_general(lax.all_gather(conv_grad, 'head', axis=1, tiled=True), w_...]
    unnamed x11 -> x22, local copies, waits for them, and re-layouts: 6.11 us -> 10.4 us
  transfers between devices with their start and end apart: 2 -> 0, of which waited for: 1 -> 0; matrix products, arithmetic and copies ran while one was open for 12% -> 0% of each run, Pallas kernels for 0% -> 0%
where the time goes in v2:
time: 70.4 us; the launch traced here: 69.6 us
  Pallas kernels  58.6 us (83%)
  local copies, waits for them, and re-layouts  10.4 us (15%)
    pallas_call x1, Pallas kernels, gather_multiply(): pl.pallas_call(gather_kernel, out_shape=(jax.ShapeDtypeStruct((rows, feat...  32.1 us
    pallas_call x1, Pallas kernels, exchange(): pl.pallas_call(exchange_kernel, out_shape=jax.ShapeDtypeStruct((count,) +...  13.3 us
    unnamed x22, local copies, waits for them, and re-layouts  10.4 us
    pallas_call x1, Pallas kernels, local(): pl.pallas_call(main_kernel, out_shape=(jax.ShapeDtypeStruct((rows, width)...  9.43 us
    pallas_call x1, Pallas kernels, local(): pl.pallas_call(head_kernel, out_shape=jax.ShapeDtypeStruct((modes, subs,...  3.8 us

profile of v2, /device:TPU:0, one launch (start us, length us, event | category | flops | bytes accessed | tf_op | source)
XLA Modules:
  0.0 69.6 jit_solution(6891001494923857918)
XLA Ops:
  0.6 0.0 copy-start
  0.6 1.1 %copy-done = bf16[384,1024]{1,0:T(8,128)(2,1)S(1)} copy-done((bf16[384,1024]{1,0:T(8,128)(2,1)S(1)}, bf16[384,1024]{1,0:T(8,128)(2,1)}, u32[]{:S(2)}) %copy-start) | copy-done | bytes 786456
  1.8 0.0 copy-start.4
  1.8 0.8 %copy-done.4 = f32[16,1024]{1,0:T(8,128)S(1)} copy-done((f32[16,1024]{1,0:T(8,128)S(1)}, f32[16,1024]{1,0:T(8,128)}, u32[]{:S(2)}) %copy-start.4) | copy-done | bytes 65560
  2.6 0.0 copy-start.8
  2.6 0.7 copy-done.8
  3.3 3.8 %head_state.1.head_ref = f32[16,8,128]{2,1,0:T(8,128)S(1)} custom-call(s32[1536]{0:T(1024)S(1)} %copy-done.8, bf16[384,1024]{1,0:T(8,128)(2,1)S(1)} %copy-done, f32[16,1024]{1,0:T(8,128)S(1)} %copy-done.4), custom_call_target="tpu_custom_call" | custom-call | tf_op jit(solution)/shard_map/head_state/pallas_call | solution.py:346
  7.1 0.0 copy-start.6
  7.1 0.6 copy-done.6
  7.7 13.3 %head_exchange.1.heads_ref = f32[4,16,8,128]{3,2,1,0:T(8,128)} custom-call(f32[16,8,128]{2,1,0:T(8,128)} %copy-done.6), custom_call_target="tpu_custom_call" | custom-call | tf_op jit(solution)/shard_map/head_exchange/pallas_call | solution.py:293
  21.0 0.0 copy-start.1
  21.0 1.1 %copy-done.1 = bf16[384,1024]{1,0:T(8,128)(2,1)S(1)} copy-done((bf16[384,1024]{1,0:T(8,128)(2,1)S(1)}, bf16[384,1024]{1,0:T(8,128)(2,1)}, u32[]{:S(2)}) %copy-start.1) | copy-done | bytes 786456
  22.2 0.0 copy-start.2
  22.2 0.9 %copy-done.2 = f32[4,16,8,128]{3,2,1,0:T(8,128)S(1)} copy-done((f32[4,16,8,128]{3,2,1,0:T(8,128)S(1)}, f32[4,16,8,128]{3,2,1,0:T(8,128)}, u32[]{:S(2)}) %copy-start.2) | copy-done | bytes 262168
  23.1 0.0 copy-start.3
  23.1 1.1 %copy-done.3 = bf16[384,1024]{1,0:T(8,128)(2,1)S(1)} copy-done((bf16[384,1024]{1,0:T(8,128)(2,1)S(1)}, bf16[384,1024]{1,0:T(8,128)(2,1)}, u32[]{:S(2)}) %copy-start.3) | copy-done | bytes 786456
  24.2 0.0 copy-start.5
  24.2 0.8 %copy-done.5 = f32[16,1024]{1,0:T(8,128)S(1)} copy-done((f32[16,1024]{1,0:T(8,128)S(1)}, f32[16,1024]{1,0:T(8,128)}, u32[]{:S(2)}) %copy-start.5) | copy-done | bytes 65560
  25.1 0.0 copy-start.7
  25.1 0.8 %copy-done.7 = f32[16,1024]{1,0:T(8,128)S(1)} copy-done((f32[16,1024]{1,0:T(8,128)S(1)}, f32[16,1024]{1,0:T(8,128)}, u32[]{:S(2)}) %copy-start.7) | copy-done | bytes 65560
  25.9 0.0 copy-start.9
  25.9 0.7 copy-done.9
  26.6 9.4 %adjoint_scan.1 = (bf16[384,1024]{1,0:T(8,128)(2,1)S(1)}, f32[16,1024]{1,0:T(8,128)S(1)}) custom-call(s32[1536]{0:T(1024)S(1)} %copy-done.9, bf16[384,1024]{1,0:T(8,128)(2,1)S(1)} %copy-done.1, bf16[384,1024]{1,0:T(8,128)(2,1)S(1)} %copy-done.3, f32[16,1024]{1,0:T(8,128)S(1)} %copy-done.7, f32[16,1024]{1,0:T(8,128)S(1)} %copy-done.5, ...), custom_call_target="tpu_custom_call" | custom-call | tf_op jit(solution)/shard_map/adjoint_scan/pallas_call | solution.py:356
  36.1 32.1 %gather_multiply.1 = (bf16[384,1024]{1,0:T(8,128)(2,1)S(1)}, f32[16,1024]{1,0:T(8,128)S(1)}) custom-call(bf16[384,1024]{1,0:T(8,128)(2,1)S(1)} %get-tuple-element.4.conv_ref, bf16[1024,8192]{1,0:T(8,128)(2,1)} %w_ref.1, f32[16,1024]{1,0:T(8,128)S(1)} %get-tuple-element.5.part_ref), custom_call_target="tpu_custom_call" | custom-call | flops 6442450944 | bytes 16777216 | tf_op jit(solution)/shard_map/gather_multiply/pallas_call | solution.py:309
  68.1 0.9 %copy.10 = bf16[384,1024]{1,0:T(8,128)(2,1)} copy(bf16[384,1024]{1,0:T(8,128)(2,1)S(1)} %get-tuple-element.8) | data formatting | bytes 1572864
  69.0 0.6 copy.11
Async XLA Ops:
  0.6 1.1 %copy-start = (bf16[384,1024]{1,0:T(8,128)(2,1)S(1)}, bf16[384,1024]{1,0:T(8,128)(2,1)}, u32[]{:S(2)}) copy-start(bf16[384,1024]{1,0:T(8,128)(2,1)} %grad_ref.3) | copy-start | bytes 2359300
  1.8 0.8 %copy-start.4 = (f32[16,1024]{1,0:T(8,128)S(1)}, f32[16,1024]{1,0:T(8,128)}, u32[]{:S(2)}) copy-start(f32[16,1024]{1,0:T(8,128)} %rate_ref.3) | copy-start | bytes 196612
  2.6 0.7 %copy-start.8 = (s32[1536]{0:T(1024)S(1)}, s32[1536]{0:T(1024)}, u32[]{:S(2)}) copy-start(s32[1536]{0:T(1024)} %seg_ref.3) | copy-start | bytes 18436
  7.1 0.6 copy-start.6
  21.0 1.1 %copy-start.1 = (bf16[384,1024]{1,0:T(8,128)(2,1)S(1)}, bf16[384,1024]{1,0:T(8,128)(2,1)}, u32[]{:S(2)}) copy-start(bf16[384,1024]{1,0:T(8,128)(2,1)} %grad_ref.3) | copy-start | bytes 2359300
  22.2 0.9 %copy-start.2 = (f32[4,16,8,128]{3,2,1,0:T(8,128)S(1)}, f32[4,16,8,128]{3,2,1,0:T(8,128)}, u32[]{:S(2)}) copy-start(f32[4,16,8,128]{3,2,1,0:T(8,128)} %head_exchange.1.heads_ref) | copy-start | bytes 786436
  23.1 1.1 %copy-start.3 = (bf16[384,1024]{1,0:T(8,128)(2,1)S(1)}, bf16[384,1024]{1,0:T(8,128)(2,1)}, u32[]{:S(2)}) copy-start(bf16[384,1024]{1,0:T(8,128)(2,1)} %input_ref.1) | copy-start | bytes 2359300
  24.2 0.8 %copy-start.5 = (f32[16,1024]{1,0:T(8,128)S(1)}, f32[16,1024]{1,0:T(8,128)}, u32[]{:S(2)}) copy-start(f32[16,1024]{1,0:T(8,128)} %rate_ref.3) | copy-start | bytes 196612
  25.1 0.8 %copy-start.7 = (f32[16,1024]{1,0:T(8,128)S(1)}, f32[16,1024]{1,0:T(8,128)}, u32[]{:S(2)}) copy-start(f32[16,1024]{1,0:T(8,128)} %residue_ref.1) | copy-start | bytes 196612
  25.9 0.7 %copy-start.9 = (s32[1536]{0:T(1024)S(1)}, s32[1536]{0:T(1024)}, u32[]{:S(2)}) copy-start(s32[1536]{0:T(1024)} %seg_ref.3) | copy-start | bytes 18436

commit v3 on v2

--- a/solution.py
+++ b/solution.py
@@ -146,12 +146,16 @@
         pl.when(place + d < count)(copies[d - 1].wait_recv)
 
 
-def gather_kernel(
-    conv_ref, w_ref, part_ref, out_ref, filter_ref,
+def fused_kernel(
+    seg_ref, grad_hbm, input_hbm, residue_hbm, rate_hbm, w_ref, out_ref, filter_ref,
+    grad_ref, input_ref, residue_ref, rate_ref, conv_ref, part_ref, head_ref, heads_ref,
+    grad_scr, input_scr, conv_scr, mode_scr, through_scr, decay_scr, residue_scr, carry_scr,
     blocks, weights, total, parts,
-    send_sem, recv_sem, weight_sem, part_send, part_recv,
+    send_sem, recv_sem, weight_sem, part_send, part_recv, head_send, head_recv, load_sem,
 ):
     rows, width = conv_ref.shape
+    modes = rate_ref.shape[0]
+    subs = width // LANES
     half = rows // 2
     count = parts.shape[0]
     place = lax.axis_index("ctx")
@@ -164,6 +168,13 @@
     def apart(k):
         return me + sum(steps[bit] for bit in steps if k & bit)
 
+    operands = []
+    for i, (src, dst) in enumerate((
+        (grad_hbm, grad_ref), (rate_hbm, rate_ref),
+        (input_hbm, input_ref), (residue_hbm, residue_ref),
+    )):
+        operands.append(pltpu.make_async_copy(src, dst, load_sem.at[i]))
+        operands[i].start()
     loads = []
     for k in range(8):
         loads.append(pltpu.make_async_copy(
@@ -179,7 +190,78 @@
     for d in range(1, count):
         other = lax.rem(place + d, count)
         pl.semaphore_signal(barrier, inc=1, device_id={"ctx": other}, device_id_type=MESH)
+
+    start = place * rows
+    zero = jnp.zeros((subs, LANES), jnp.float32)
+    operands[0].wait()
+    spread(grad_ref, grad_scr, wide)
+    operands[1].wait()
+    fill_decay(rate_ref, mode_scr, decay_scr)
+
+    def head_step(i, state):
+        t = rows - 1 - i
+        link = link_at(seg_ref, start + t)
+        grad = grad_scr[pl.ds(t, subs, stride=rows), :]
+        return tuple(grad + decay_scr[link, m] * state[m] for m in range(modes))
+
+    state = lax.fori_loop(0, rows, head_step, (zero,) * modes, unroll=8)
+    for m in range(modes):
+        head_ref[m] = state[m]
     pl.semaphore_wait(barrier, 3 + count - 1)
+    copies = []
+    for d in range(1, count):
+        copies.append(pltpu.make_async_remote_copy(
+            src_ref=head_ref,
+            dst_ref=heads_ref.at[d],
+            send_sem=head_send.at[d],
+            recv_sem=head_recv.at[d],
+            device_id={"ctx": jnp.maximum(place - d, 0)},
+            device_id_type=MESH,
+        ))
+    for d in range(1, count):
+        pl.when(place >= d)(copies[d - 1].start)
+
+    spread(rate_ref, mode_scr, lambda v: jnp.exp(-rows * v))
+    for m in range(modes):
+        through_scr[m] = mode_scr[pl.ds(m, subs, stride=modes), :]
+    operands[2].wait()
+    spread(input_ref, input_scr, wide)
+    operands[3].wait()
+    spread(residue_ref, mode_scr, lambda v: v)
+    for m in range(modes):
+        residue_scr[m] = mode_scr[pl.ds(m, subs, stride=modes), :]
+    carry_scr[...] = jnp.zeros_like(carry_scr)
+    last = seg_ref.shape[0] - 1
+
+    def hop(d):
+        copies[d - 1].wait_recv()
+        source = place + d
+        same = seg_ref[source * rows] == seg_ref[jnp.minimum((source + 1) * rows, last)]
+        linked = jnp.where(same, 1.0, 0.0)
+        carry_scr[...] = heads_ref[d] + linked * through_scr[...] * carry_scr[...]
+
+    for d in range(count - 1, 0, -1):
+        pl.when(place + d < count)(functools.partial(hop, d))
+
+    def step(i, state):
+        values, sums = state
+        t = rows - 1 - i
+        link = link_at(seg_ref, start + t)
+        grad = grad_scr[pl.ds(t, subs, stride=rows), :]
+        inputs = input_scr[pl.ds(t, subs, stride=rows), :]
+        values = tuple(grad + decay_scr[link, m] * values[m] for m in range(modes))
+        sums = tuple(sums[m] + inputs * values[m] for m in range(modes))
+        terms = [residue_scr[m] * values[m] for m in range(modes)]
+        while len(terms) > 1:
+            terms = [a + b for a, b in zip(terms[::2], terms[1::2])]
+        conv_scr[pl.ds(t, subs, stride=rows), :] = terms[0]
+        return values, sums
+
+    def round_rows(first):
+        for tile in range(subs):
+            conv_ref[pl.ds(first, half), pl.ds(tile * LANES, LANES)] = conv_scr[
+                pl.ds(tile * rows + first, half), :
+            ].astype(conv_ref.dtype)
 
     def piece(k, h):
         if k == 0:
@@ -218,12 +300,20 @@
 
         lax.fori_loop(0, total.shape[1] // 256, tile, 0)
 
+    state = (tuple(carry_scr[m] for m in range(modes)), (zero,) * modes)
+    state = lax.fori_loop(0, half, step, state, unroll=4)
+    round_rows(half)
+    send(0, 1, 2)
+    send(0, 1, 4)
+    send(0, 1, 1)
+    _, state = lax.fori_loop(half, rows, step, state, unroll=4)
+    round_rows(0)
     send(0, 0, 2)
-    send(0, 1, 4)
-    send(0, 1, 2)
     send(0, 0, 4)
     send(0, 0, 1)
-    send(0, 1, 1)
+    for m in range(modes):
+        mode_scr[pl.ds(m, subs, stride=modes), :] = state[m]
+    fold(mode_scr, part_ref, lambda v: v)
     sums = []
     for d in range(1, count):
         other = lax.rem(place + d, count)
@@ -239,50 +329,50 @@
     parts[0] = part_ref[...]
     loads[0].wait()
     multiply(0, 0, rows)
-    sent[1, 0].wait_recv()
-    sent[1, 1].wait_recv()
-    loads[1].wait()
-    multiply(1, 0, rows)
-    sent[2, 0].wait_recv()
-    send(2, 0, 4)
-    send(2, 0, 1)
     sent[4, 1].wait_recv()
     send(4, 1, 2)
     send(4, 1, 1)
-    for k in (2, 3, 4, 5):
+    sent[2, 1].wait_recv()
+    send(2, 1, 1)
+    for k in (1, 2, 3, 4, 5):
         loads[k].wait()
-    multiply(2, 0, half)
+    sent[1, 1].wait_recv()
+    sent[1, 0].wait_recv()
+    multiply(1, 0, rows)
     multiply(4, half, half)
-    sent[3, 0].wait_recv()
-    multiply(3, 0, half)
+    multiply(2, half, half)
     sent[5, 1].wait_recv()
     multiply(5, half, half)
+    sent[3, 1].wait_recv()
+    multiply(3, half, half)
     for copy in sums:
         copy.wait()
     value = parts[lax.rem(count - place, count)]
     for z in range(1, count):
         value = value + parts[lax.rem(z + count - place, count)]
     filter_ref[...] = value
-    sent[2, 1].wait_recv()
-    send(2, 1, 1)
+    sent[2, 0].wait_recv()
+    send(2, 0, 4)
+    send(2, 0, 1)
     sent[4, 0].wait_recv()
     send(4, 0, 1)
-    multiply(2, half, half)
+    multiply(2, 0, half)
     multiply(4, 0, half)
-    sent[3, 1].wait_recv()
-    multiply(3, half, half)
+    sent[3, 0].wait_recv()
+    multiply(3, 0, half)
     sent[5, 0].wait_recv()
     multiply(5, 0, half)
-    sent[6, 0].wait_recv()
-    send(6, 0, 1)
-    sent[6, 1].wait_recv()
-    send(6, 1, 1)
     loads[6].wait()
-    multiply(6, 0, rows)
-    sent[7, 0].wait_recv()
-    sent[7, 1].wait_recv()
     loads[7].wait()
-    multiply(7, 0, rows)
+    for h in (1, 0):
+        sent[6, h].wait_recv()
+        send(6, h, 1)
+        multiply(6, h * half, half)
+    for h in (1, 0):
+        sent[7, h].wait_recv()
+        multiply(7, h * half, half)
+    for d in range(1, count):
+        pl.when(place >= d)(copies[d - 1].wait_send)
     for copy in sent.values():
         copy.wait_send()
     out_ref[...] = total[...].astype(out_ref.dtype)
@@ -301,39 +391,56 @@
     )(head)
 
 
-def gather_multiply(conv_grad, w_in, partial):
-    rows, width = conv_grad.shape
+def fused(out_grad, conv_input, residues, decay_rate, segments, w_in):
+    rows, width = out_grad.shape
+    modes = residues.shape[0]
     features = w_in.shape[0]
+    subs = width // LANES
     count = lax.axis_size("ctx")
     dma = pltpu.SemaphoreType.DMA
+    f32, bf16 = jnp.float32, jnp.bfloat16
+    tall = pltpu.VMEM((rows * subs, LANES), f32)
+    packed = pltpu.VMEM((modes, subs, LANES), f32)
+    block = pltpu.VMEM((rows, width), bf16)
+    small = pltpu.VMEM((modes, width), f32)
     return pl.pallas_call(
-        gather_kernel,
+        fused_kernel,
         out_shape=(
-            jax.ShapeDtypeStruct((rows, features), jnp.bfloat16),
-            jax.ShapeDtypeStruct(partial.shape, partial.dtype),
+            jax.ShapeDtypeStruct((rows, features), bf16),
+            jax.ShapeDtypeStruct((modes, width), f32),
         ),
-        in_specs=[VMEM, pl.BlockSpec(memory_space=pl.ANY), VMEM],
+        in_specs=[SMEM] + [pl.BlockSpec(memory_space=pl.ANY)] * 5,
         out_specs=(VMEM, VMEM),
         scratch_shapes=[
-            pltpu.VMEM((7, rows, width), jnp.bfloat16),
-            pltpu.VMEM((8, features, width), jnp.bfloat16),
-            pltpu.VMEM((rows, features), jnp.float32),
-            pltpu.VMEM((count,) + partial.shape, partial.dtype),
+            block, block, small, small, block, small, packed,
+            pltpu.VMEM((count, modes, subs, LANES), f32),
+            tall, tall, tall,
+            pltpu.VMEM((modes * subs, LANES), f32),
+            packed,
+            pltpu.VMEM((2, modes, subs, LANES), f32),
+            packed, packed,
+            pltpu.VMEM((7, rows, width), bf16),
+            pltpu.VMEM((8, features, width), bf16),
+            pltpu.VMEM((rows, features), f32),
+            pltpu.VMEM((count, modes, width), f32),
             dma((7, 2)), dma((7, 2)), dma((8,)), dma((count,)), dma((count,)),
+            dma((count,)), dma((count,)), dma((4,)),
         ],
         compiler_params=pltpu.CompilerParams(
-            collective_id=2, has_side_effects=True, vmem_limit_bytes=44 << 20
+            collective_id=2, has_side_effects=True, vmem_limit_bytes=56 << 20
         ),
         cost_estimate=pl.CostEstimate(
             flops=16 * rows * width * features,
             bytes_accessed=16 * features * width,
             transcendentals=0,
         ),
-        name="gather_multiply",
-    )(conv_grad, w_in, partial)
+        name="fused_backward",
+    )(segments, out_grad, conv_input, residues, decay_rate, w_in)
 
 
 def local(out_grad, conv_input, residues, decay_rate, segments, w_in):
+    if lax.axis_size("head") == 8:
+        return fused(out_grad, conv_input, residues, decay_rate, segments, w_in)
     rows, width = out_grad.shape
     modes = residues.shape[0]
     subs = width // LANES
@@ -365,8 +472,6 @@
         compiler_params=params,
         name="adjoint_scan",
     )(segments, out_grad, conv_input, residues, decay_rate, heads)
-    if lax.axis_size("head") == 8:
-        return gather_multiply(conv_grad, w_in, partial)
     filter_grad = lax.psum(partial, "ctx")
     d_input = lax.dot_general(
         lax.all_gather(conv_grad, "head", axis=1, tiled=True),

time: 70.4 us -> 59.5 us (0.85)
  local copies, waits for them, and re-layouts: 10.4 us -> 3.54 us
  Pallas kernels: 58.6 us -> 55.1 us
    unnamed x22 -> x2, local copies, waits for them, and re-layouts: 10.4 us -> 3.54 us
    pallas_call x4 -> x1, Pallas kernels: 58.6 us -> 55.1 us  [fused(): pl.pallas_call(fused_kernel, out_shape=(jax.ShapeDtypeStruct((rows, featu...]
where the time goes in v3:
time: 59.5 us; the launch traced here: 59.3 us
  Pallas kernels  55.1 us (93%)
  local copies, waits for them, and re-layouts  3.54 us (6%)
  between operations  0.64 us (1%)
    pallas_call x1, Pallas kernels, fused(): pl.pallas_call(fused_kernel, out_shape=(jax.ShapeDtypeStruct((rows, featu...  55.1 us
    unnamed x2, local copies, waits for them, and re-layouts  3.54 us

profile of v3, /device:TPU:0, one launch (start us, length us, event | category | flops | bytes accessed | tf_op | source)
XLA Modules:
  0.0 59.3 jit_solution(15969585973247593755)
XLA Ops:
  0.6 55.1 %fused_backward.1 = (bf16[384,1024]{1,0:T(8,128)(2,1)}, f32[16,1024]{1,0:T(8,128)}) custom-call(s32[1536]{0:T(1024)} %seg_ref.1, bf16[384,1024]{1,0:T(8,128)(2,1)} %grad_hbm.1, bf16[384,1024]{1,0:T(8,128)(2,1)} %input_hbm.1, f32[16,1024]{1,0:T(8,128)} %residue_hbm.1, f32[16,1024]{1,0:T(8,128)} %rate_hbm.1, bf16[1024,8192]{1,0:T(8,128)(2,1)} %w_ref.1), custom_call_target="tpu_custom_call" | custom-call | flops 6442450944 | bytes 16777216 | tf_op jit(solution)/shard_map/fused_backward/pallas_call | solution.py:406
  55.8 2.1 %copy.10 = bf16[384,1024]{1,0:T(8,128)(2,1)} copy(bf16[384,1024]{1,0:T(8,128)(2,1)} %get-tuple-element.4) | data formatting | bytes 1572864
  57.8 1.5 %copy.11 = f32[16,1024]{1,0:T(8,128)} copy(f32[16,1024]{1,0:T(8,128)} %get-tuple-element.5) | data formatting | bytes 131072

commit v4 on v3

--- a/solution.py
+++ b/solution.py
@@ -156,7 +156,8 @@
     rows, width = conv_ref.shape
     modes = rate_ref.shape[0]
     subs = width // LANES
-    half = rows // 2
+    part = rows // 4
+    half = 2 * part
     count = parts.shape[0]
     place = lax.axis_index("ctx")
     me = lax.axis_index("head")
@@ -206,7 +207,8 @@
 
     state = lax.fori_loop(0, rows, head_step, (zero,) * modes, unroll=8)
     for m in range(modes):
-        head_ref[m] = state[m]
+        mode_scr[pl.ds(m * subs, subs), :] = state[m]
+    head_ref[...] = mode_scr[...].astype(head_ref.dtype)
     pl.semaphore_wait(barrier, 3 + count - 1)
     copies = []
     for d in range(1, count):
@@ -223,7 +225,7 @@
 
     spread(rate_ref, mode_scr, lambda v: jnp.exp(-rows * v))
     for m in range(modes):
-        through_scr[m] = mode_scr[pl.ds(m, subs, stride=modes), :]
+        through_scr[pl.ds(m * subs, subs), :] = mode_scr[pl.ds(m, subs, stride=modes), :]
     operands[2].wait()
     spread(input_ref, input_scr, wide)
     operands[3].wait()
@@ -238,7 +240,7 @@
         source = place + d
         same = seg_ref[source * rows] == seg_ref[jnp.minimum((source + 1) * rows, last)]
         linked = jnp.where(same, 1.0, 0.0)
-        carry_scr[...] = heads_ref[d] + linked * through_scr[...] * carry_scr[...]
+        carry_scr[...] = wide(heads_ref[d]) + linked * through_scr[...] * carry_scr[...]
 
     for d in range(count - 1, 0, -1):
         pl.when(place + d < count)(functools.partial(hop, d))
@@ -259,14 +261,14 @@
 
     def round_rows(first):
         for tile in range(subs):
-            conv_ref[pl.ds(first, half), pl.ds(tile * LANES, LANES)] = conv_scr[
-                pl.ds(tile * rows + first, half), :
+            conv_ref[pl.ds(first, part), pl.ds(tile * LANES, LANES)] = conv_scr[
+                pl.ds(tile * rows + first, part), :
             ].astype(conv_ref.dtype)
 
     def piece(k, h):
         if k == 0:
-            return conv_ref.at[pl.ds(h * half, half)]
-        return blocks.at[k - 1, pl.ds(h * half, half)]
+            return conv_ref.at[pl.ds(h * part, part)]
+        return blocks.at[k - 1, pl.ds(h * part, part)]
 
     sent = {}
 
@@ -300,17 +302,18 @@
 
         lax.fori_loop(0, total.shape[1] // 256, tile, 0)
 
-    state = (tuple(carry_scr[m] for m in range(modes)), (zero,) * modes)
-    state = lax.fori_loop(0, half, step, state, unroll=4)
-    round_rows(half)
-    send(0, 1, 2)
-    send(0, 1, 4)
-    send(0, 1, 1)
-    _, state = lax.fori_loop(half, rows, step, state, unroll=4)
-    round_rows(0)
-    send(0, 0, 2)
-    send(0, 0, 4)
-    send(0, 0, 1)
+    state = (
+        tuple(carry_scr[pl.ds(m * subs, subs), :] for m in range(modes)),
+        (zero,) * modes,
+    )
+    for h in (3, 2, 1, 0):
+        done = (3 - h) * part
+        state = lax.fori_loop(done, done + part, step, state, unroll=4)
+        round_rows(h * part)
+        send(0, h, 2)
+        send(0, h, 4)
+        send(0, h, 1)
+    state = state[1]
     for m in range(modes):
         mode_scr[pl.ds(m, subs, stride=modes), :] = state[m]
     fold(mode_scr, part_ref, lambda v: v)
@@ -329,48 +332,53 @@
     parts[0] = part_ref[...]
     loads[0].wait()
     multiply(0, 0, rows)
-    sent[4, 1].wait_recv()
-    send(4, 1, 2)
-    send(4, 1, 1)
-    sent[2, 1].wait_recv()
-    send(2, 1, 1)
     for k in (1, 2, 3, 4, 5):
         loads[k].wait()
-    sent[1, 1].wait_recv()
-    sent[1, 0].wait_recv()
+
+    def pass_on(h):
+        sent[2, h].wait_recv()
+        sent[4, h].wait_recv()
+        if h % 2:
+            send(2, h, 4)
+        else:
+            send(4, h, 2)
+        send(2, h, 1)
+        send(4, h, 1)
+
+    def lower(k, first):
+        for h in (1, 0):
+            sent[k, first + h].wait_recv()
+        multiply(k, first * part, half)
+
+    pass_on(3)
+    for h in (3, 2, 1, 0):
+        sent[1, h].wait_recv()
     multiply(1, 0, rows)
+    pass_on(2)
+    multiply(2, half, half)
     multiply(4, half, half)
-    multiply(2, half, half)
-    sent[5, 1].wait_recv()
-    multiply(5, half, half)
-    sent[3, 1].wait_recv()
-    multiply(3, half, half)
+    lower(3, 2)
+    lower(5, 2)
     for copy in sums:
         copy.wait()
     value = parts[lax.rem(count - place, count)]
     for z in range(1, count):
         value = value + parts[lax.rem(z + count - place, count)]
     filter_ref[...] = value
-    sent[2, 0].wait_recv()
-    send(2, 0, 4)
-    send(2, 0, 1)
-    sent[4, 0].wait_recv()
-    send(4, 0, 1)
+    pass_on(1)
+    pass_on(0)
     multiply(2, 0, half)
     multiply(4, 0, half)
-    sent[3, 0].wait_recv()
-    multiply(3, 0, half)
-    sent[5, 0].wait_recv()
-    multiply(5, 0, half)
+    lower(3, 0)
+    lower(5, 0)
     loads[6].wait()
     loads[7].wait()
-    for h in (1, 0):
-        sent[6, h].wait_recv()
-        send(6, h, 1)
-        multiply(6, h * half, half)
-    for h in (1, 0):
-        sent[7, h].wait_recv()
-        multiply(7, h * half, half)
+    for first in (2, 0):
+        for h in (1, 0):
+            sent[6, first + h].wait_recv()
+            send(6, first + h, 1)
+        multiply(6, first * part, half)
+        lower(7, first)
     for d in range(1, count):
         pl.when(place >= d)(copies[d - 1].wait_send)
     for copy in sent.values():
@@ -401,6 +409,7 @@
     f32, bf16 = jnp.float32, jnp.bfloat16
     tall = pltpu.VMEM((rows * subs, LANES), f32)
     packed = pltpu.VMEM((modes, subs, LANES), f32)
+    flat = pltpu.VMEM((modes * subs, LANES), f32)
     block = pltpu.VMEM((rows, width), bf16)
     small = pltpu.VMEM((modes, width), f32)
     return pl.pallas_call(
@@ -412,18 +421,18 @@
         in_specs=[SMEM] + [pl.BlockSpec(memory_space=pl.ANY)] * 5,
         out_specs=(VMEM, VMEM),
         scratch_shapes=[
-            block, block, small, small, block, small, packed,
-            pltpu.VMEM((count, modes, subs, LANES), f32),
+            block, block, small, small, block, small,
+            pltpu.VMEM((modes * subs, LANES), bf16),
+            pltpu.VMEM((count, modes * subs, LANES), bf16),
             tall, tall, tall,
-            pltpu.VMEM((modes * subs, LANES), f32),
-            packed,
+            flat, flat,
             pltpu.VMEM((2, modes, subs, LANES), f32),
-            packed, packed,
+            packed, flat,
             pltpu.VMEM((7, rows, width), bf16),
             pltpu.VMEM((8, features, width), bf16),
             pltpu.VMEM((rows, features), f32),
             pltpu.VMEM((count, modes, width), f32),
-            dma((7, 2)), dma((7, 2)), dma((8,)), dma((count,)), dma((count,)),
+            dma((7, 4)), dma((7, 4)), dma((8,)), dma((count,)), dma((count,)),
             dma((count,)), dma((count,)), dma((4,)),
         ],
         compiler_params=pltpu.CompilerParams(

time: 59.5 us -> 54.5 us (0.916)
  Pallas kernels: 55.1 us -> 50.1 us
    pallas_call x1, Pallas kernels: 55.1 us -> 50.1 us  [fused(): pl.pallas_call(fused_kernel, out_shape=(jax.ShapeDtypeStruct((rows, featu...]
where the time goes in v4:
time: 54.5 us; the launch traced here: 54.3 us
  Pallas kernels  50.1 us (92%)
  local copies, waits for them, and re-layouts  3.54 us (6%)
  between operations  0.64 us (1%)
    pallas_call x1, Pallas kernels, fused(): pl.pallas_call(fused_kernel, out_shape=(jax.ShapeDtypeStruct((rows, featu...  50.1 us
    unnamed x2, local copies, waits for them, and re-layouts  3.54 us

profile of v4, /device:TPU:0, one launch (start us, length us, event | category | flops | bytes accessed | tf_op | source)
XLA Modules:
  0.0 54.3 jit_solution(11589663767004153157)
XLA Ops:
  0.6 50.1 %fused_backward.1 = (bf16[384,1024]{1,0:T(8,128)(2,1)}, f32[16,1024]{1,0:T(8,128)}) custom-call(s32[1536]{0:T(1024)} %seg_ref.1, bf16[384,1024]{1,0:T(8,128)(2,1)} %grad_hbm.1, bf16[384,1024]{1,0:T(8,128)(2,1)} %input_hbm.1, f32[16,1024]{1,0:T(8,128)} %residue_hbm.1, f32[16,1024]{1,0:T(8,128)} %rate_hbm.1, bf16[1024,8192]{1,0:T(8,128)(2,1)} %w_ref.1), custom_call_target="tpu_custom_call" | custom-call | flops 6442450944 | bytes 16777216 | tf_op jit(solution)/shard_map/fused_backward/pallas_call | solution.py:415
  50.7 2.1 %copy.10 = bf16[384,1024]{1,0:T(8,128)(2,1)} copy(bf16[384,1024]{1,0:T(8,128)(2,1)} %get-tuple-element.4) | data formatting | bytes 1572864
  52.8 1.5 %copy.11 = f32[16,1024]{1,0:T(8,128)} copy(f32[16,1024]{1,0:T(8,128)} %get-tuple-element.5) | data formatting | bytes 131072

commit v5 on v4

--- a/solution.py
+++ b/solution.py
@@ -15,8 +15,10 @@
 
 def spread(src, dst, convert):
     rows, width = src.shape
-    for tile in range(width // LANES):
-        dst[pl.ds(tile * rows, rows), :] = convert(src[:, pl.ds(tile * LANES, LANES)])
+    tiles = width // LANES
+    pitch = dst.shape[0] // tiles
+    for tile in range(tiles):
+        dst[pl.ds(tile * pitch, rows), :] = convert(src[:, pl.ds(tile * LANES, LANES)])
 
 
 def fold(src, dst, convert):
@@ -158,6 +160,7 @@
     subs = width // LANES
     part = rows // 4
     half = 2 * part
+    pitch = grad_scr.shape[0] // subs
     count = parts.shape[0]
     place = lax.axis_index("ctx")
     me = lax.axis_index("head")
@@ -202,7 +205,7 @@
     def head_step(i, state):
         t = rows - 1 - i
         link = link_at(seg_ref, start + t)
-        grad = grad_scr[pl.ds(t, subs, stride=rows), :]
+        grad = grad_scr[pl.ds(t, subs, stride=pitch), :]
         return tuple(grad + decay_scr[link, m] * state[m] for m in range(modes))
 
     state = lax.fori_loop(0, rows, head_step, (zero,) * modes, unroll=8)
@@ -249,20 +252,20 @@
         values, sums = state
         t = rows - 1 - i
         link = link_at(seg_ref, start + t)
-        grad = grad_scr[pl.ds(t, subs, stride=rows), :]
-        inputs = input_scr[pl.ds(t, subs, stride=rows), :]
+        grad = grad_scr[pl.ds(t, subs, stride=pitch), :]
+        inputs = input_scr[pl.ds(t, subs, stride=pitch), :]
         values = tuple(grad + decay_scr[link, m] * values[m] for m in range(modes))
         sums = tuple(sums[m] + inputs * values[m] for m in range(modes))
         terms = [residue_scr[m] * values[m] for m in range(modes)]
         while len(terms) > 1:
             terms = [a + b for a, b in zip(terms[::2], terms[1::2])]
-        conv_scr[pl.ds(t, subs, stride=rows), :] = terms[0]
+        conv_scr[pl.ds(t, subs, stride=pitch), :] = terms[0]
         return values, sums
 
     def round_rows(first):
         for tile in range(subs):
             conv_ref[pl.ds(first, part), pl.ds(tile * LANES, LANES)] = conv_scr[
-                pl.ds(tile * rows + first, part), :
+                pl.ds(tile * pitch + first, part), :
             ].astype(conv_ref.dtype)
 
     def piece(k, h):
@@ -308,7 +311,7 @@
     )
     for h in (3, 2, 1, 0):
         done = (3 - h) * part
-        state = lax.fori_loop(done, done + part, step, state, unroll=4)
+        state = lax.fori_loop(done, done + part, step, state, unroll=8)
         round_rows(h * part)
         send(0, h, 2)
         send(0, h, 4)
@@ -407,7 +410,7 @@
     count = lax.axis_size("ctx")
     dma = pltpu.SemaphoreType.DMA
     f32, bf16 = jnp.float32, jnp.bfloat16
-    tall = pltpu.VMEM((rows * subs, LANES), f32)
+    tall = pltpu.VMEM(((rows + 8) * subs, LANES), f32)
     packed = pltpu.VMEM((modes, subs, LANES), f32)
     flat = pltpu.VMEM((modes * subs, LANES), f32)
     block = pltpu.VMEM((rows, width), bf16)
@@ -422,8 +425,8 @@
         out_specs=(VMEM, VMEM),
         scratch_shapes=[
             block, block, small, small, block, small,
-            pltpu.VMEM((modes * subs, LANES), bf16),
-            pltpu.VMEM((count, modes * subs, LANES), bf16),
+            flat,
+            pltpu.VMEM((count, modes * subs, LANES), f32),
             tall, tall, tall,
             flat, flat,
             pltpu.VMEM((2, modes, subs, LANES), f32),

time: 54.5 us -> 55.6 us (1.020)
  Pallas kernels: 50.1 us -> 51.1 us
    pallas_call x1, Pallas kernels: 50.1 us -> 51.1 us  [fused(): pl.pallas_call(fused_kernel, out_shape=(jax.ShapeDtypeStruct((rows, featu...]
where the time goes in v5:
time: 55.6 us; the launch traced here: 55.3 us
  Pallas kernels  51.1 us (92%)
  local copies, waits for them, and re-layouts  3.54 us (6%)
  between operations  0.64 us (1%)
    pallas_call x1, Pallas kernels, fused(): pl.pallas_call(fused_kernel, out_shape=(jax.ShapeDtypeStruct((rows, featu...  51.1 us
    unnamed x2, local copies, waits for them, and re-layouts  3.54 us

profile of v5, /device:TPU:0, one launch (start us, length us, event | category | flops | bytes accessed | tf_op | source)
XLA Modules:
  0.0 55.3 jit_solution(8626134339815337731)
XLA Ops:
  0.6 51.1 %fused_backward.1 = (bf16[384,1024]{1,0:T(8,128)(2,1)}, f32[16,1024]{1,0:T(8,128)}) custom-call(s32[1536]{0:T(1024)} %seg_ref.1, bf16[384,1024]{1,0:T(8,128)(2,1)} %grad_hbm.1, bf16[384,1024]{1,0:T(8,128)(2,1)} %input_hbm.1, f32[16,1024]{1,0:T(8,128)} %residue_hbm.1, f32[16,1024]{1,0:T(8,128)} %rate_hbm.1, bf16[1024,8192]{1,0:T(8,128)(2,1)} %w_ref.1), custom_call_target="tpu_custom_call" | custom-call | flops 6442450944 | bytes 16777216 | tf_op jit(solution)/shard_map/fused_backward/pallas_call | solution.py:418
  51.8 2.1 %copy.10 = bf16[384,1024]{1,0:T(8,128)(2,1)} copy(bf16[384,1024]{1,0:T(8,128)(2,1)} %get-tuple-element.4) | data formatting | bytes 1572864
  53.9 1.5 %copy.11 = f32[16,1024]{1,0:T(8,128)} copy(f32[16,1024]{1,0:T(8,128)} %get-tuple-element.5) | data formatting | bytes 131072

commit v6 on v5

--- a/solution.py
+++ b/solution.py
@@ -149,10 +149,10 @@
 
 
 def fused_kernel(
-    seg_ref, grad_hbm, input_hbm, residue_hbm, rate_hbm, w_ref, out_ref, filter_ref,
+    seg_ref, grad_hbm, input_hbm, residue_hbm, rate_hbm, w_ref, total, filter_ref,
     grad_ref, input_ref, residue_ref, rate_ref, conv_ref, part_ref, head_ref, heads_ref,
     grad_scr, input_scr, conv_scr, mode_scr, through_scr, decay_scr, residue_scr, carry_scr,
-    blocks, weights, total, parts,
+    blocks, weights, parts,
     send_sem, recv_sem, weight_sem, part_send, part_recv, head_send, head_recv, load_sem,
 ):
     rows, width = conv_ref.shape
@@ -364,10 +364,11 @@
     lower(5, 2)
     for copy in sums:
         copy.wait()
-    value = parts[lax.rem(count - place, count)]
-    for z in range(1, count):
-        value = value + parts[lax.rem(z + count - place, count)]
-    filter_ref[...] = value
+    for i, places in enumerate((range(count // 2), range(count // 2, count))):
+        value = jnp.zeros((modes, width), jnp.float32)
+        for z in places:
+            value = value + parts[lax.rem(z + count - place, count)]
+        filter_ref[i] = value
     pass_on(1)
     pass_on(0)
     multiply(2, 0, half)
@@ -386,7 +387,6 @@
         pl.when(place >= d)(copies[d - 1].wait_send)
     for copy in sent.values():
         copy.wait_send()
-    out_ref[...] = total[...].astype(out_ref.dtype)
 
 
 def exchange(head):
@@ -418,8 +418,8 @@
     return pl.pallas_call(
         fused_kernel,
         out_shape=(
-            jax.ShapeDtypeStruct((rows, features), bf16),
-            jax.ShapeDtypeStruct((modes, width), f32),
+            jax.ShapeDtypeStruct((rows, features), f32),
+            jax.ShapeDtypeStruct((2, modes, width), f32),
         ),
         in_specs=[SMEM] + [pl.BlockSpec(memory_space=pl.ANY)] * 5,
         out_specs=(VMEM, VMEM),
@@ -433,7 +433,6 @@
             packed, flat,
             pltpu.VMEM((7, rows, width), bf16),
             pltpu.VMEM((8, features, width), bf16),
-            pltpu.VMEM((rows, features), f32),
             pltpu.VMEM((count, modes, width), f32),
             dma((7, 4)), dma((7, 4)), dma((8,)), dma((count,)), dma((count,)),
             dma((count,)), dma((count,)), dma((4,)),
@@ -452,7 +451,8 @@
 
 def local(out_grad, conv_input, residues, decay_rate, segments, w_in):
     if lax.axis_size("head") == 8:
-        return fused(out_grad, conv_input, residues, decay_rate, segments, w_in)
+        total, halves = fused(out_grad, conv_input, residues, decay_rate, segments, w_in)
+        return total.astype(jnp.bfloat16), halves[0] + halves[1]
     rows, width = out_grad.shape
     modes = residues.shape[0]
     subs = width // LANES

time: 55.6 us -> 56.2 us (1.011)
  other arithmetic: 0 us -> 3.92 us
  local copies, waits for them, and re-layouts: 3.54 us -> 0 us
    unnamed x2 -> x0, local copies, waits for them, and re-layouts: 3.54 us -> none
    convert_element_type x0 -> x1, other arithmetic: none -> 2.41 us  [local(): return (total.astype(jnp.bfloat16), halves[0] + halves[1])]
    add x0 -> x1, other arithmetic: none -> 1.51 us  [local(): return (total.astype(jnp.bfloat16), halves[0] + halves[1])]
where the time goes in v6:
time: 56.2 us; the launch traced here: 55.9 us
  Pallas kernels  51.4 us (91%)
  other arithmetic  3.92 us (7%)
  between operations  0.64 us (1%)
    pallas_call x1, Pallas kernels, fused(): pl.pallas_call(fused_kernel, out_shape=(jax.ShapeDtypeStruct((rows, featu...  51.4 us
    convert_element_type x1, other arithmetic, local(): return (total.astype(jnp.bfloat16), halves[0] + halves[1])  2.41 us
    add x1, other arithmetic, local(): return (total.astype(jnp.bfloat16), halves[0] + halves[1])  1.51 us

profile of v6, /device:TPU:0, one launch (start us, length us, event | category | flops | bytes accessed | tf_op | source)
XLA Modules:
  0.0 55.9 jit_solution(8750665384230107621)
XLA Ops:
  0.6 51.4 %fused_backward.1 = (f32[384,1024]{1,0:T(8,128)}, f32[2,16,1024]{2,1,0:T(8,128)}) custom-call(s32[1536]{0:T(1024)} %seg_ref.1, bf16[384,1024]{1,0:T(8,128)(2,1)} %grad_hbm.1, bf16[384,1024]{1,0:T(8,128)(2,1)} %input_hbm.1, f32[16,1024]{1,0:T(8,128)} %residue_hbm.1, f32[16,1024]{1,0:T(8,128)} %rate_hbm.1, bf16[1024,8192]{1,0:T(8,128)(2,1)} %w_ref.1), custom_call_target="tpu_custom_call" | custom-call | flops 6442450944 | bytes 16777216 | tf_op jit(solution)/shard_map/fused_backward/pallas_call | solution.py:418
  52.0 2.4 %convert_element_type.3 = bf16[384,1024]{1,0:T(8,128)(2,1)} convert(f32[384,1024]{1,0:T(8,128)} %get-tuple-element.4) | non-fusion elementwise | flops 393216 | bytes 2359296 | tf_op jit(solution)/shard_map/convert_element_type | solution.py:455
  54.4 1.5 %add_bitcast_fusion = f32[16,1024]{1,0:T(8,128)} fusion(f32[2,16,1024]{2,1,0:T(8,128)} %get-tuple-element.5), kind=kLoop, calls=%fused_computation | loop fusion | flops 16384 | bytes 196608 | tf_op jit(solution)/shard_map/add | solution.py:455
